TPU v7x, 256 devices: a whole 4x4x8 slice. The times are simulated.
256 devices in a mesh: space: 16 (over z, core), ray: 16 (over x, y).
Axes of the slice: x: 4, y: 4, z: 8, core: 2. Of those that a mesh axis runs over, the one named last changes fastest.
Arguments:
- grid_table: bfloat16 [16, 4096, 256], P('space'), may hold values from -6 to 6
- weights: bfloat16 [16, 4, 256, 256], P('space'), may hold values from -0.375 to 0.375
- biases: float32 [16, 4, 256], P('space'), may hold values from -1.5 to 1.5
- density_head: float32 [16, 256], P('space'), may hold values from -0.375 to 0.375
- sample_cells: int32 [16, 8192, 8], P('space', 'ray'), may hold values from 0 to 4095
- sample_counts: int32 [8192, 16], P('ray', 'space'), may hold values from 0 to 8
- ray_order: int32 [8192, 16], P('ray'), may hold values from 0 to 15, each once within a row
- cotangent: float32 [8192, 256], P('ray'), may hold values from -6 to 6
Outputs:
- composite: float32 [8192, 256], P(('ray', 'space'))
- weight_grads: float32 [16, 4, 256, 256], P('space')
- bias_grads: float32 [16, 4, 256], P('space')
- head_grads: float32 [16, 256], P('space')
Inputs may be any that keep to these rules, and one draw needn't show every extreme that they name: `ray_order`: each row is a permutation of 0 .. 15: the order in which the ray meets the partitions. `sample_counts`: A count of 0 means that the ray does not touch the partition.
All inputs are finite; a program needn't handle non-finite values.
Results may differ from a plain program's by a relative error of at most 0.0065.
The roundings to bfloat16 on the way count: a program that leaves them out, or rounds other values in their place, can miss the bound.
Values sent between devices are 32-bit elements; how exact they have to be, the bound alone decides.
A program may use at most 128 MiB of HBM per device.

v0:
```python
import jax
import jax.numpy as jnp
from jax import lax
from jax.sharding import PartitionSpec as P

step_length = 0.05


def gather_turned(arrays, axis, dims):
    turned = [jnp.moveaxis(a, dim, 0) for a, dim in zip(arrays, dims)]
    widths = [t[0].size for t in turned]
    both = jnp.concatenate([t.reshape(-1, w) for t, w in zip(turned, widths)], axis=1)
    whole = lax.all_gather(both, axis, axis=0, tiled=True)
    tiles = jnp.split(whole, [sum(widths[:k]) for k in range(1, len(widths))], axis=1)
    return tuple(
        (
            jnp.moveaxis(b.reshape(-1, *t.shape[1:]), 0, dim)
            for b, t, dim in zip(tiles, turned, dims)
        )
    )


def in_blocks(shard, dim, peers):
    before, after = (shard.shape[:dim], shard.shape[dim + 1 :])
    return jnp.moveaxis(shard.reshape(*before, peers, -1, *after), dim, 0)


def sent_and_summed(shard, axis, dim):
    peers = lax.axis_size(axis)
    tiles = lax.all_to_all(in_blocks(shard, dim, peers), axis, 0, 0, tiled=True)
    return jnp.sum(tiles, axis=0)


def forward(table, layer_mats, layer_bias, cells):
    hidden = table[cells.reshape(-1)]
    layer_inputs = []
    pre_acts = []
    linear = None
    for layer in range(layer_mats.shape[0]):
        layer_inputs.append(hidden)
        linear = (
            jnp.dot(hidden, layer_mats[layer], preferred_element_type=jnp.float32)
            + layer_bias[layer]
        )
        pre_acts.append(linear)
        if layer + 1 < layer_mats.shape[0]:
            hidden = jax.nn.relu(linear).astype(jnp.bfloat16)
    return (layer_inputs, pre_acts, linear)


def segment(features, head, count):
    slots = count.shape[0]
    width = features.shape[1]
    samples = features.shape[0] // slots
    logits = jnp.dot(features, head, precision=lax.Precision.HIGHEST)
    density = jax.nn.softplus(logits).reshape(slots, samples)
    live = lax.iota(jnp.int32, samples)[None, :] < count[:, None]
    optical = jnp.where(live, density * step_length, jnp.float32(0.0))
    before = jnp.cumsum(optical, axis=1) - optical
    blend = jnp.exp(-before) * (1.0 - jnp.exp(-optical))
    colour = jnp.einsum(
        "rs,rsw->rw",
        blend,
        features.reshape(slots, samples, width),
        precision=lax.Precision.HIGHEST,
    )
    decay = -jnp.sum(optical, axis=1)
    return (colour, decay)


def on_device(
    grid_table, weights, biases, density_head, sample_cells, sample_counts, ray_order, cotangent
):
    table = grid_table[0]
    layer_mats = weights[0]
    layer_bias = biases[0]
    head = density_head[0]
    count = sample_counts[:, 0]
    own_index = lax.axis_index("space")
    parts = lax.axis_size("space")
    layer_inputs, pre_acts, features = forward(table, layer_mats, layer_bias, sample_cells[0])
    outputs, pull = jax.vjp(
        lambda feats, weight_head: segment(feats, weight_head, count), features, head
    )
    colour, decay = outputs
    product = jnp.sum(colour * cotangent, axis=1)
    select = lax.iota(jnp.int32, parts)[None, :] == own_index
    own_rank = jnp.sum(jnp.where(select, ray_order, 0), axis=1)
    later = ray_order > own_rank[:, None]
    decays, products = gather_turned((decay[:, None], product[:, None]), "space", (1, 1))
    before_all = ray_order[:, None, :] < ray_order[:, :, None]
    prefix_all = jnp.exp(
        jnp.sum(jnp.where(before_all, decays[:, None, :], jnp.float32(0.0)), axis=2)
    )
    shares = prefix_all * products
    prefix = jnp.sum(jnp.where(select, prefix_all, jnp.float32(0.0)), axis=1)
    tail = jnp.sum(jnp.where(later, shares, jnp.float32(0.0)), axis=1)
    composite = sent_and_summed(prefix[:, None] * colour, "space", 0)
    grad_features, grad_head = pull((prefix[:, None] * cotangent, tail))
    grad_linear = grad_features
    mats = []
    offsets = []
    for layer in range(layer_mats.shape[0] - 1, -1, -1):
        grad_half = grad_linear.astype(jnp.bfloat16)
        mat_grad = lax.dot_general(
            layer_inputs[layer],
            grad_half,
            (((0,), (0,)), ((), ())),
            preferred_element_type=jnp.float32,
        )
        offset_grad = jnp.sum(grad_linear, axis=0)
        if layer > 0:
            back = lax.dot_general(
                grad_half,
                layer_mats[layer],
                (((1,), (1,)), ((), ())),
                preferred_element_type=jnp.float32,
            )
            grad_linear = back * (pre_acts[layer - 1] > 0).astype(jnp.float32)
        mats.append(mat_grad)
        offsets.append(offset_grad)
    weight_grads = jnp.stack(mats[::-1])
    bias_grads = jnp.stack(offsets[::-1])
    weight_grads, bias_grads, grad_head = lax.psum((weight_grads, bias_grads, grad_head), "ray")
    return (composite, weight_grads[None], bias_grads[None], grad_head[None])


def solution(mesh):
    placed = (
        P("space", None, None),
        P("space", None, None, None),
        P("space", None, None),
        P("space", None),
        P("space", "ray", None),
        P("ray", "space"),
        P("ray", None),
        P("ray", None),
    )
    return jax.shard_map(
        on_device,
        mesh=mesh,
        in_specs=placed,
        out_specs=(
            P(("ray", "space"), None),
            P("space", None, None, None),
            P("space", None, None),
            P("space", None),
        ),
        check_vma=False,
    )
```

profile of v0, /device:TPU:8, one launch (start us, length us, event | category | flops | bytes accessed | tf_op | source)
XLA Modules:
  0.0 197.4 jit_solution(2402974236432176873)
XLA Ops:
  9.2 16.9 %gather_fusion = bf16[4096,256]{1,0:T(8,128)(2,1)} fusion(bf16[4096,256]{1,0:T(8,128)(2,1)S(1)} %bitcast.111, s32[4096]{0:T(1024)S(1)} %broadcast_clamp_fusion), kind=kCustom, calls=%fused_computation | custom fusion | bytes 4210688 | tf_op jit(solution)/shard_map/gather | solution.py:35
  26.1 2.3 %convolution_add_fusion.3 = f32[4096,256]{1,0:T(8,128)S(1)} fusion(bf16[4096,256]{1,0:T(8,128)(2,1)} %gather_fusion, f32[256]{0:T(256)S(1)} %bitcast.125, bf16[1,4,256,256]{3,2,1,0:T(8,128)(2,1)S(1)} %copy-done.13), kind=kOutput, calls=%fused_computation.7 | convolution fusion | flops 537919488 | bytes 6423552 | tf_op jit(solution)/shard_map/dot_general | solution.py:42
  29.2 1.2 copy-done.5
  31.1 1.3 copy-done.3
  33.1 1.2 copy-done.7
  34.3 1.9 copy-done.1
  36.3 3.6 %fusion.54 = f32[1,4096]{1,0:T(1,128)S(1)} fusion(f32[4096,256]{1,0:T(8,128)S(1)} %convolution_add_fusion, f32[1,256]{1,0:T(1,128)S(1)} %copy-done.17), kind=kOutput, calls=%fused_computation.85 | convolution fusion | flops 12582912 | bytes 4211712 | tf_op jit(solution)/shard_map/jvp()/dot_general | solution.py:55
  40.7 6.3 %fusion.2 = f32[512,1,256]{2,1,0:T(1,128)S(1)} fusion(f32[512,8,1]{1,2,0:T(1,128)S(1)} %bitcast.113, f32[4096,256]{1,0:T(8,128)} %copy-done.1), kind=kOutput, calls=%fused_computation.11 | convolution fusion | flops 12582912 | bytes 4734976 | tf_op jit(solution)/shard_map/jvp(rs,rsw->rw)/dot_general | solution.py:61
  47.2 20.3 %all-gather = f32[16,1,1024]{2,1,0:T(1,128)S(1)} all-gather(f32[1,1,1024]{2,1,0:T(1,128)S(1)} %maximum_bitcast_fusion.1), channel_id=1, replica_groups=mesh['space'=16,'ray'=16] {'space'}, dimensions={0}, use_global_device_ids=true | all-gather | bytes 69632 | tf_op jit(solution)/shard_map/all_gather | solution.py:13
  68.8 4.2 %fusion = f32[512,1,8]{2,1,0:T(1,128)S(1)} fusion(f32[4096,256]{1,0:T(8,128)S(1)} %copy-done.2, f32[512,256,1]{1,0,2:T(8,128)S(1)} %bitcast.112), kind=kOutput, calls=%fused_computation.9 | convolution fusion | flops 12582912 | bytes 4734976 | tf_op jit(solution)/shard_map/transpose(jvp(rs,rsw->rw))/dot_general | solution.py:61
  74.5 1.9 reduce_window_sum.23
  76.4 1.9 select_multiply_fusion
  78.3 1.1 reshape.88
  79.5 4.6 %fusion.22 = f32[1,256,256]{2,1,0:T(8,128)S(1)} fusion(f32[256]{0:T(256)S(1)} %bitcast.130, f32[4096]{0:T(1024)S(1)} %fusion.52, f32[512,256]{1,0:T(8,128)S(1)} %get-tuple-element.14, f32[512,8]{1,0:T(8,128)S(1)} %subtract_multiply_fusion, f32[4096,256]{1,0:T(8,128)} %copy-done.7), kind=kOutput, calls=%fused_computation.30 | convolution fusion | flops 543162368 | bytes 5014528 | tf_op jit(solution)/shard_map/dot_general | solution.py:105
  84.2 2.0 fusion.65
  88.1 1.1 copy-done.6
  90.0 1.0 fusion.67
  92.4 1.0 maximum_bitcast_fusion
  93.4 3.8 %all-to-all-start = ((f32[16,32,256]{2,1,0:T(8,128)}), f32[16,32,256]{2,1,0:T(8,128)S(1)}, u32[]{:S(2)}, u32[]{:S(2)}) async-start(f32[16,32,256]{2,1,0:T(8,128)} %bitcast.22), calls=%async_computation | async-start | bytes 1048576 | tf_op jit(solution)/shard_map/all_to_all | solution.py:30
  97.3 3.4 %fusion.4 = f32[256]{0:T(256)S(1)} fusion(f32[256]{0:T(256)S(1)} %bitcast.132, f32[4096]{0:T(1024)S(1)} %fusion.52, f32[512,256]{1,0:T(8,128)S(1)} %get-tuple-element.14, f32[512,8]{1,0:T(8,128)S(1)} %subtract_multiply_fusion), kind=kLoop, calls=%fused_computation.13 | loop fusion | flops 4194048 | bytes 559104 | tf_op jit(solution)/shard_map/reduce_sum | solution.py:111
  100.7 4.1 %fusion.68 = f32[1,256]{1,0:T(1,128)S(1)} fusion(f32[4096,1]{0,1:T(1,128)S(1)} %bitcast.118, f32[4096,256]{1,0:T(8,128)} %copy-done.1), kind=kOutput, calls=%fused_computation.99 | convolution fusion | flops 12582912 | bytes 4211712 | tf_op jit(solution)/shard_map/transpose(jvp())/dot_general | solution.py:55
  104.8 37.6 %all-reduce = (f32[1,4,256]{2,1,0:T(4,128)}, f32[1,256]{1,0:T(1,128)}) all-reduce(f32[1,4,256]{2,1,0:T(4,128)S(1)} %maximum_bitcast_fusion.2, f32[1,256]{1,0:T(1,128)S(1)} %fusion.68), channel_id=1, replica_groups=mesh['space'=16,'ray'=16] {'ray'}, use_global_device_ids=true, to_apply=%region_14.15 | all-reduce | flops 1280 | bytes 10240 | tf_op jit(solution)/shard_map/psum | solution.py:124
  143.0 45.2 %all-reduce.3.cloned.1.call-done = f32[1,4,256,256]{3,2,1,0:T(8,128)} async-done(((f32[1,4,256,256]{3,2,1,0:T(8,128)}), f32[1,4,256,256]{3,2,1,0:T(8,128)}) %all-reduce.3.cloned.1.call-update) | async-done | bytes 1048592 | tf_op jit(solution)/shard_map/psum | solution.py:124
  188.3 2.3 %copy.36 = f32[1,4,256,256]{3,2,1,0:T(8,128)} copy(f32[1,4,256,256]{3,2,1,0:T(8,128)} %all-reduce.3.cloned.1.call-done) | data formatting | bytes 2097152
  (66 shorter events, 12.5 us)
Async XLA Ops:
  7.2 2.0 %copy-start = (bf16[1,4096,256]{2,1,0:T(8,128)(2,1)S(1)}, bf16[1,4096,256]{2,1,0:T(8,128)(2,1)}, u32[]{:S(2)}) copy-start(bf16[1,4096,256]{2,1,0:T(8,128)(2,1)} %param.8) | copy-start | bytes 6291460
  7.2 181.1 %all-reduce.3.cloned.1.call-start = ((), (), s32[]{:S(2)}) async-start(), calls=%async_computation.1 | async-start | bytes 2097152 | tf_op jit(solution)/shard_map/psum | solution.py:124
  9.2 16.9 %copy-start.13 = (bf16[1,4,256,256]{3,2,1,0:T(8,128)(2,1)S(1)}, bf16[1,4,256,256]{3,2,1,0:T(8,128)(2,1)}, u32[]{:S(2)}) copy-start(bf16[1,4,256,256]{3,2,1,0:T(8,128)(2,1)} %param.9) | copy-start | bytes 1572868
  28.4 2.0 copy-start.5
  30.4 2.0 %copy-start.3 = (f32[4096,256]{1,0:T(8,128)}, f32[4096,256]{1,0:T(8,128)S(1)}, u32[]{:S(2)}) copy-start(f32[4096,256]{1,0:T(8,128)S(1)} %convolution_add_fusion.2) | copy-start | bytes 12582916
  32.4 2.0 copy-start.7
  32.4 3.9 %copy-start.17 = (f32[1,256]{1,0:T(1,128)S(1)}, f32[1,256]{1,0:T(1,128)}, u32[]{:S(2)}) copy-start(f32[1,256]{1,0:T(1,128)} %param.11) | copy-start | bytes 3076
  34.3 1.9 copy-start.1
  36.3 3.8 %copy-start.16 = (s32[512,1]{0,1:T(1,128)S(1)}, s32[512,1]{0,1:T(1,128)}, u32[]{:S(2)}) copy-start(s32[512,1]{0,1:T(1,128)} %param.13) | copy-start | bytes 6148
  39.9 7.2 %copy-start.11 = (f32[512,256]{1,0:T(8,128)S(1)}, f32[512,256]{1,0:T(8,128)}, u32[]{:S(2)}) copy-start(f32[512,256]{1,0:T(8,128)} %param.15) | copy-start | bytes 1572868
  39.9 27.6 %copy-start.15 = (s32[512,16]{0,1:T(8,128)S(1)}, s32[512,16]{0,1:T(8,128)}, u32[]{:S(2)}) copy-start(s32[512,16]{0,1:T(8,128)} %param.14) | copy-start | bytes 98308
  40.6 27.3 %copy-start.12 = (f32[512,256]{1,0:T(8,128)S(1)}, f32[512,256]{1,0:T(8,128)}, u32[]{:S(2)}) copy-start(f32[512,256]{1,0:T(8,128)} %param.15) | copy-start | bytes 1572868
  40.7 28.1 %copy-start.2 = (f32[4096,256]{1,0:T(8,128)S(1)}, f32[4096,256]{1,0:T(8,128)}, u32[]{:S(2)}) copy-start(f32[4096,256]{1,0:T(8,128)} %copy-done.1) | copy-start | bytes 12582916
  73.0 0.7 copy-start.10
  78.3 5.8 %copy-start.14 = (bf16[1,4,256,256]{3,2,1,0:T(8,128)(2,1)S(1)}, bf16[1,4,256,256]{3,2,1,0:T(8,128)(2,1)}, u32[]{:S(2)}) copy-start(bf16[1,4,256,256]{3,2,1,0:T(8,128)(2,1)} %param.9) | copy-start | bytes 1572868
  79.5 4.7 %copy-start.8 = (f32[4096,256]{1,0:T(8,128)S(1)}, f32[4096,256]{1,0:T(8,128)}, u32[]{:S(2)}) copy-start(f32[4096,256]{1,0:T(8,128)} %copy-done.7) | copy-start | bytes 12582916
  84.2 2.2 %copy-start.4 = (f32[4096,256]{1,0:T(8,128)S(1)}, f32[4096,256]{1,0:T(8,128)}, u32[]{:S(2)}) copy-start(f32[4096,256]{1,0:T(8,128)} %copy-done.3) | copy-start | bytes 12582916
  87.1 2.2 %copy-start.6 = (f32[4096,256]{1,0:T(8,128)S(1)}, f32[4096,256]{1,0:T(8,128)}, u32[]{:S(2)}) copy-start(f32[4096,256]{1,0:T(8,128)} %copy-done.5) | copy-start | bytes 12582916
  90.0 1.6 copy-start.9
  93.4 49.0 %all-to-all-start = ((f32[16,32,256]{2,1,0:T(8,128)}), f32[16,32,256]{2,1,0:T(8,128)S(1)}, u32[]{:S(2)}, u32[]{:S(2)}) async-start(f32[16,32,256]{2,1,0:T(8,128)} %bitcast.22), calls=%async_computation | async-start | bytes 1048576 | tf_op jit(solution)/shard_map/all_to_all | solution.py:30
Sparse Core Ops, SparseCore 0:
  93.6 94.6 all-reduce.2
where the time goes:
time: 198 us; the launch traced here: 197 us
  blocking collectives  57.9 us (29%)
  waiting for transfers between devices  45.2 us (23%)
  matrix products  33.5 us (17%)
  local copies, waits for them, and re-layouts  30.8 us (16%)
  between operations  14.4 us (7%)
  other arithmetic  11.7 us (6%)
  starting transfers between devices  3.88 us (2%)
    psum x1, waiting for transfers between devices, on_device(): lax.psum((weight_grads, bias_grads, grad_head), 'ray')  45.2 us
    psum x1, blocking collectives, on_device(): lax.psum((weight_grads, bias_grads, grad_head), 'ray')  37.6 us
    all_gather x1, blocking collectives, gather_turned(): whole = lax.all_gather(both, axis, axis=0, tiled=True)  20.3 us
    gather x1, local copies, waits for them, and re-layouts, forward(): hidden = table[cells.reshape(-1)]  16.9 us
    unnamed x39, local copies, waits for them, and re-layouts  11.5 us
    dot_general x2, matrix products, segment(): jnp.einsum('rs,rsw->rw', blend, features.reshape(slots, samples, width),...  10.5 us
    dot_general x2, matrix products, segment(): logits = jnp.dot(features, head, precision=lax.Precision.HIGHEST)  7.69 us
    dot_general x4, matrix products, on_device(): lax.dot_general(layer_inputs[layer], grad_half, (((0,), (0,)), ((), ())),...  6.86 us
  transfers between devices with their start and end apart: 2, of which 1 were waited for; matrix products, arithmetic and copies ran while one was open for 4% of the time, Pallas kernels for 0%

commit v1 on v0

v1 whole, which is shorter than its diff:
```python
import jax
import jax.numpy as jnp
from jax import lax
from jax.experimental import pallas as pl
from jax.experimental.pallas import tpu as pltpu
from jax.sharding import PartitionSpec as P

MESH = pl.DeviceIdType.MESH
f32 = jnp.float32
bf16 = jnp.bfloat16

STEP = 0.05
W = 256
LAYERS = 4
SLOTS = 8
CELLS = 4096
LANES = 128
RAYS = 512
GROUPS = RAYS // LANES
GROUP = SLOTS * LANES
SAMPLES = RAYS * SLOTS
WIDE = 2
CHUNKS = GROUPS // WIDE
CHUNK = WIDE * GROUP
PARTS = 16
SIDE = 4
BLOCK = W // 2 // SIDE
UNROLL = 32


def dot(a, b, ca, cb):
    return lax.dot_general(a, b, (((ca,), (cb,)), ((), ())), preferred_element_type=f32)


def scan_down(v, row):
    for k in (1, 2, 4):
        v = v + jnp.where(row >= k, pltpu.roll(v, k, 0), 0.0)
    return v


def scan_up(v, row):
    for k in (1, 2, 4):
        v = v + jnp.where(row < SLOTS - k, pltpu.roll(v, SLOTS - k, 0), 0.0)
    return v


def kernel(
    cells, table, w, bias, head, counts, ranks, cot,
    comp_out, dw_out, bias_out, head_out,
    table32, rows32, x16, wt, cols, cot_t, hid, feat, grad, seg, colour, colour_rows,
    packed, gathered, comp_in, dw, col_sums, small, small_x, small_y,
    red, in1, in2,
    ag_send, ag_recv, comp_send, comp_recv, sends, recvs, small_send, small_recv,
):
    space = lax.axis_index("space")
    ray = lax.axis_index("ray")
    spot = (ray // SIDE, ray % SIDE)

    def ray_peer(axis, d):
        there = lax.rem(spot[axis] + d, SIDE)
        return there, {"ray": there * SIDE + spot[1] if axis == 0 else spot[0] * SIDE + there}

    barrier = pltpu.get_barrier_semaphore()
    for d in range(1, PARTS):
        pl.semaphore_signal(
            barrier, inc=1, device_id={"space": lax.rem(space + d, PARTS)}, device_id_type=MESH
        )
    for axis in (0, 1):
        for d in range(1, SIDE):
            pl.semaphore_signal(
                barrier, inc=1, device_id=ray_peer(axis, d)[1], device_id_type=MESH
            )

    def widen(k, _):
        part = table[pl.ds(pl.multiple_of(k * 512, 512), 512), :].astype(f32)
        table32[pl.ds(pl.multiple_of(k * 512, 512), 512), 0, :] = part[:, :LANES]
        table32[pl.ds(pl.multiple_of(k * 512, 512), 512), 1, :] = part[:, LANES:]
        return 0

    lax.fori_loop(0, CELLS // 512, widen, 0)

    def pick(k, _):
        base = k * UNROLL
        got = [table32[cells[base + u]] for u in range(UNROLL)]
        for u in range(UNROLL):
            rows32[base + u] = got[u]
        return 0

    lax.fori_loop(0, SAMPLES // UNROLL, pick, 0)

    for layer in range(LAYERS):
        wt[layer] = w[layer].T
    cols[...] = jnp.concatenate([bias[...], head[...], jnp.zeros((3, W), f32)], axis=0).T
    cot_t[...] = cot[...].T
    slot_row = lax.broadcasted_iota(jnp.int32, (SLOTS, LANES), 0)
    ones = jnp.ones((1, LANES), f32)
    head_col = cols[:, LAYERS : LAYERS + 1] * ones

    def forward(c, _):
        start = pl.multiple_of(c * CHUNK, CHUNK)
        low = rows32[pl.ds(start, CHUNK), 0, :]
        high = rows32[pl.ds(start, CHUNK), 1, :]
        x = jnp.concatenate([low, high], axis=1).astype(bf16)
        x16[c] = x
        value = None
        for layer in range(LAYERS):
            value = dot(wt[layer], x, 1, 1 if layer == 0 else 0) + cols[:, layer : layer + 1]
            if layer + 1 < LAYERS:
                x = jnp.maximum(value, 0.0).astype(bf16)
                hid[layer, c] = x
        feat[c] = value
        return 0

    lax.fori_loop(0, CHUNKS, forward, 0)

    decay_rows, product_rows = [], []
    for g in range(GROUPS):
        lanes = slice(g * LANES, (g + 1) * LANES)
        turned = cot_t[:, lanes]
        logit, along = [], []
        for s in range(SLOTS):
            at = (g % WIDE) * GROUP + s * LANES
            f = feat[g // WIDE, :, at : at + LANES]
            logit.append(jnp.sum(f * head_col, axis=0, keepdims=True))
            along.append(jnp.sum(f * turned, axis=0, keepdims=True))
        logit = jnp.concatenate(logit, axis=0)
        along = jnp.concatenate(along, axis=0)
        live = slot_row < counts[g : g + 1, :]
        density = jnp.maximum(logit, 0.0) + jnp.log1p(jnp.exp(-jnp.abs(logit)))
        optical = jnp.where(live, density * STEP, 0.0)
        total = scan_down(optical, slot_row)
        through = jnp.exp(-(total - optical))
        past = jnp.exp(-optical)
        blend = through * (1.0 - past)
        share = blend * along
        after = scan_up(share, slot_row)
        seg[g, 0] = blend
        seg[g, 1] = along * through * past - (after - share)
        seg[g, 2] = jnp.where(live, STEP / (1.0 + jnp.exp(-logit)), 0.0)
        decay_rows.append(-total[SLOTS - 1 : SLOTS, :])
        product_rows.append(after[0:1, :])
    packed[...] = jnp.concatenate(decay_rows + product_rows, axis=0)

    pl.semaphore_wait(barrier, PARTS - 1 + 2 * (SIDE - 1))
    mine = pl.multiple_of(space * 8, 8)

    def ag_copy(d):
        return pltpu.make_async_remote_copy(
            src_ref=packed,
            dst_ref=gathered.at[pl.ds(mine, 8), :],
            send_sem=ag_send.at[d],
            recv_sem=ag_recv.at[d],
            device_id={"space": lax.rem(space + d, PARTS)},
            device_id_type=MESH,
        )

    for d in range(1, PARTS):
        ag_copy(d).start()
    gathered[pl.ds(mine, 8), :] = packed[...]

    def blend_colours(g, _):
        c = g // WIDE
        at = pl.multiple_of((g % WIDE) * GROUP, GROUP)
        blend = seg[g, 0]
        acc = None
        for s in range(SLOTS):
            term = feat[c, :, pl.ds(at + s * LANES, LANES)] * blend[s : s + 1, :]
            acc = term if acc is None else acc + term
        colour[g] = acc
        return 0

    lax.fori_loop(0, GROUPS, blend_colours, 0)
    for d in range(1, PARTS):
        ag_copy(d).wait_recv()

    decay = jnp.concatenate(
        [gathered[pl.ds(g, PARTS, stride=8), :] for g in range(GROUPS)], axis=1
    )
    product = jnp.concatenate(
        [gathered[pl.ds(GROUPS + g, PARTS, stride=8), :] for g in range(GROUPS)], axis=1
    )
    rank = ranks[...]
    earlier = jnp.zeros((PARTS, RAYS), f32)
    for q in range(PARTS):
        earlier = earlier + jnp.where(rank[q : q + 1, :] < rank, decay[q : q + 1, :], 0.0)
    prefixes = jnp.exp(earlier)
    own = lax.broadcasted_iota(jnp.int32, (PARTS, RAYS), 0) == space
    own_rank = jnp.sum(jnp.where(own, rank, 0), axis=0, keepdims=True)
    prefix = jnp.sum(jnp.where(own, prefixes, 0.0), axis=0, keepdims=True)
    tail = jnp.sum(jnp.where(rank > own_rank, prefixes * product, 0.0), axis=0, keepdims=True)

    for g in range(GROUPS):
        lanes = slice(g * LANES, (g + 1) * LANES)
        colour_rows[lanes, :] = (colour[g] * prefix[:, lanes]).T
    kept = RAYS // PARTS

    def comp_copy(d):
        there = lax.rem(space + d, PARTS)
        return pltpu.make_async_remote_copy(
            src_ref=colour_rows.at[pl.ds(pl.multiple_of(there * kept, kept), kept), :],
            dst_ref=comp_in.at[space],
            send_sem=comp_send.at[d],
            recv_sem=comp_recv.at[d],
            device_id={"space": there},
            device_id_type=MESH,
        )

    for d in range(1, PARTS):
        comp_copy(d).start()

    head_sum = jnp.zeros((W, LANES), f32)
    last_sum = jnp.zeros((W, LANES), f32)
    for g in range(GROUPS):
        lanes = slice(g * LANES, (g + 1) * LANES)
        pull = cot_t[:, lanes] * prefix[:, lanes]
        blend = seg[g, 0]
        slope = seg[g, 2] * (prefix[:, lanes] * seg[g, 1] - tail[:, lanes])
        for s in range(SLOTS):
            at = (g % WIDE) * GROUP + s * LANES
            d_logit = slope[s : s + 1, :]
            grads = pull * blend[s : s + 1, :] + head_col * d_logit
            head_sum = head_sum + feat[g // WIDE, :, at : at + LANES] * d_logit
            last_sum = last_sum + grads
            grad[g // WIDE, :, at : at + LANES] = grads.astype(bf16)
    col_sums[LAYERS] = head_sum
    col_sums[LAYERS - 1] = last_sum

    def phase1(layer, half, d):
        there, device = ray_peer(half, d)
        return pltpu.make_async_remote_copy(
            src_ref=dw.at[
                layer, pl.ds(pl.multiple_of(half * (W // 2) + there * BLOCK, BLOCK), BLOCK), :
            ],
            dst_ref=in1.at[layer, half, d],
            send_sem=sends.at[0, layer, half, d],
            recv_sem=recvs.at[0, layer, half, d],
            device_id=device,
            device_id_type=MESH,
        )

    def phase2(layer, half, d):
        return pltpu.make_async_remote_copy(
            src_ref=red.at[layer, half],
            dst_ref=in2.at[layer, half, spot[1 - half]],
            send_sem=sends.at[1, layer, half, d],
            recv_sem=recvs.at[1, layer, half, d],
            device_id=ray_peer(1 - half, d)[1],
            device_id_type=MESH,
        )

    def own_rows(half):
        return pl.ds(pl.multiple_of(half * (W // 2) + spot[half] * BLOCK, BLOCK), BLOCK)

    def phase3(layer, half, d):
        rows = dw_out.at[layer, own_rows(half), :]
        return pltpu.make_async_remote_copy(
            src_ref=rows,
            dst_ref=rows,
            send_sem=sends.at[2, layer, half, d],
            recv_sem=recvs.at[2, layer, half, d],
            device_id=ray_peer(half, d)[1],
            device_id_type=MESH,
        )

    def small_copy(axis, d):
        return pltpu.make_async_remote_copy(
            src_ref=(small, small_x.at[SIDE])[axis],
            dst_ref=(small_x, small_y)[axis].at[spot[axis]],
            send_sem=small_send.at[axis, d],
            recv_sem=small_recv.at[axis, d],
            device_id=ray_peer(axis, d)[1],
            device_id_type=MESH,
        )

    for layer in range(LAYERS - 1, -1, -1):
        for c in range(CHUNKS):
            if layer > 0:
                term = dot(hid[layer - 1, c], grad[c], 1, 1)
            else:
                term = dot(grad[c], x16[c], 1, 0)
            total = term if c == 0 else total + term
        dw[layer] = total if layer > 0 else total.T
        for d in range(1, SIDE):
            for half in (0, 1):
                phase1(layer, half, d).start()
        if layer > 0:
            def back(c, acc):
                pulled = jnp.where(hid[layer - 1, c] > 0, dot(w[layer], grad[c], 1, 0), 0.0)
                grad[c] = pulled.astype(bf16)
                for t in range(CHUNK // LANES):
                    acc = acc + pulled[:, t * LANES : (t + 1) * LANES]
                return acc

            acc = jnp.zeros((W, LANES), f32)
            for c in range(CHUNKS):
                acc = back(c, acc)
            col_sums[layer - 1] = acc

    lane = lax.broadcasted_iota(jnp.int32, (W, LANES), 1)
    gathered_cols = jnp.zeros((W, LANES), f32)
    for k in range(LAYERS + 1):
        gathered_cols = jnp.where(
            lane == k, jnp.sum(col_sums[k], axis=1, keepdims=True), gathered_cols
        )
    small[...] = gathered_cols.T[:8, :]
    for d in range(1, SIDE):
        small_copy(0, d).start()

    order = range(LAYERS - 1, -1, -1)
    for layer in order:
        for half in (0, 1):
            total = dw[layer, own_rows(half), :]
            for d in range(1, SIDE):
                phase1(layer, half, d).wait_recv()
                total = total + in1[layer, half, d]
            red[layer, half] = total
            in2[layer, half, spot[1 - half]] = total
            for d in range(1, SIDE):
                phase2(layer, half, d).start()

    small_x[spot[0]] = small[...]
    for d in range(1, SIDE):
        small_copy(0, d).wait_recv()
    small_x[SIDE] = (small_x[0] + small_x[1]) + (small_x[2] + small_x[3])
    for d in range(1, SIDE):
        small_copy(1, d).start()

    for layer in order:
        for half in (0, 1):
            for d in range(1, SIDE):
                phase2(layer, half, d).wait_recv()
            total = (in2[layer, half, 0] + in2[layer, half, 1]) + (
                in2[layer, half, 2] + in2[layer, half, 3]
            )
            dw_out[layer, own_rows(half), :] = total
            for d in range(1, SIDE):
                phase3(layer, half, d).start()

    small_y[spot[1]] = small_x[SIDE]
    for d in range(1, SIDE):
        small_copy(1, d).wait_recv()
    summed = (small_y[0] + small_y[1]) + (small_y[2] + small_y[3])
    bias_out[...] = summed[:LAYERS, :]
    head_out[...] = summed[LAYERS : LAYERS + 1, :]

    comp_in[space] = colour_rows[pl.ds(pl.multiple_of(space * kept, kept), kept), :]
    for d in range(1, PARTS):
        comp_copy(d).wait_recv()
    total = comp_in[0]
    for q in range(1, PARTS):
        total = total + comp_in[q]
    comp_out[...] = total

    for layer in order:
        for half in (0, 1):
            for d in range(1, SIDE):
                phase3(layer, half, d).wait_recv()
    for d in range(1, PARTS):
        ag_copy(d).wait_send()
        comp_copy(d).wait_send()
    for axis in (0, 1):
        for d in range(1, SIDE):
            small_copy(axis, d).wait_send()
            for layer in order:
                for phase in (phase1, phase2, phase3):
                    phase(layer, axis, d).wait_send()


def on_device(
    grid_table, weights, biases, density_head, sample_cells, sample_counts, ray_order, cotangent
):
    cells = sample_cells[0].T.reshape(SLOTS, GROUPS, LANES).transpose(1, 0, 2).reshape(SAMPLES)
    counts = sample_counts.reshape(GROUPS, LANES)
    in_vmem = pl.BlockSpec(memory_space=pltpu.VMEM)
    dma = pltpu.SemaphoreType.DMA
    composite, dw, db, dh = pl.pallas_call(
        kernel,
        out_shape=(
            jax.ShapeDtypeStruct((RAYS // PARTS, W), f32),
            jax.ShapeDtypeStruct((LAYERS, W, W), f32),
            jax.ShapeDtypeStruct((LAYERS, W), f32),
            jax.ShapeDtypeStruct((1, W), f32),
        ),
        in_specs=[pl.BlockSpec(memory_space=pltpu.SMEM)] + [in_vmem] * 7,
        out_specs=(in_vmem,) * 4,
        scratch_shapes=[
            pltpu.VMEM((CELLS, 2, LANES), f32),
            pltpu.VMEM((SAMPLES, 2, LANES), f32),
            pltpu.VMEM((CHUNKS, CHUNK, W), bf16),
            pltpu.VMEM((LAYERS, W, W), bf16),
            pltpu.VMEM((W, 8), f32),
            pltpu.VMEM((W, RAYS), f32),
            pltpu.VMEM((LAYERS - 1, CHUNKS, W, CHUNK), bf16),
            pltpu.VMEM((CHUNKS, W, CHUNK), f32),
            pltpu.VMEM((CHUNKS, W, CHUNK), bf16),
            pltpu.VMEM((GROUPS, 3, SLOTS, LANES), f32),
            pltpu.VMEM((GROUPS, W, LANES), f32),
            pltpu.VMEM((RAYS, W), f32),
            pltpu.VMEM((8, LANES), f32),
            pltpu.VMEM((PARTS * 8, LANES), f32),
            pltpu.VMEM((PARTS, RAYS // PARTS, W), f32),
            pltpu.VMEM((LAYERS, W, W), f32),
            pltpu.VMEM((LAYERS + 1, W, LANES), f32),
            pltpu.VMEM((8, W), f32),
            pltpu.VMEM((SIDE + 1, 8, W), f32),
            pltpu.VMEM((SIDE, 8, W), f32),
            pltpu.VMEM((LAYERS, 2, BLOCK, W), f32),
            pltpu.VMEM((LAYERS, 2, SIDE, BLOCK, W), f32),
            pltpu.VMEM((LAYERS, 2, SIDE, BLOCK, W), f32),
            dma((PARTS,)),
            dma((PARTS,)),
            dma((PARTS,)),
            dma((PARTS,)),
            dma((3, LAYERS, 2, SIDE)),
            dma((3, LAYERS, 2, SIDE)),
            dma((2, SIDE)),
            dma((2, SIDE)),
        ],
        compiler_params=pltpu.CompilerParams(
            collective_id=0, has_side_effects=True, vmem_limit_bytes=58 << 20
        ),
        cost_estimate=pl.CostEstimate(
            flops=22 * SAMPLES * W * W, bytes_accessed=6 << 20, transcendentals=6 * SAMPLES
        ),
    )(
        cells, grid_table[0], weights[0], biases[0], density_head, counts, ray_order.T, cotangent
    )
    return composite, dw[None], db[None], dh


def solution(mesh):
    placed = (
        P("space", None, None),
        P("space", None, None, None),
        P("space", None, None),
        P("space", None),
        P("space", "ray", None),
        P("ray", "space"),
        P("ray", None),
        P("ray", None),
    )
    return jax.shard_map(
        on_device,
        mesh=mesh,
        in_specs=placed,
        out_specs=(
            P(("ray", "space"), None),
            P("space", None, None, None),
            P("space", None, None),
            P("space", None),
        ),
        check_vma=False,
    )
```

time: 198 us -> 59.6 us (0.30)
  blocking collectives: 57.9 us -> 0 us
  Pallas kernels: 0 us -> 53.5 us
  waiting for transfers between devices: 45.2 us -> 0 us
  matrix products: 33.5 us -> 0 us
  local copies, waits for them, and re-layouts: 30.8 us -> 4.82 us
  between operations: 14.4 us -> 0.66 us
  other arithmetic: 11.7 us -> 0 us
  starting transfers between devices: 3.88 us -> 0 us
    pallas_call x0 -> x1, Pallas kernels: none -> 53.5 us  [on_device(): pl.pallas_call(kernel, out_shape=(jax.ShapeDtypeStruct((RAYS // PARTS, W)...]
    psum x1 -> x0, waiting for transfers between devices: 45.2 us -> none  [on_device(): lax.psum((weight_grads, bias_grads, grad_head), 'ray')]
    psum x1 -> x0, blocking collectives: 37.6 us -> none  [on_device(): lax.psum((weight_grads, bias_grads, grad_head), 'ray')]
    dot_general x15 -> x0, matrix products: 33.5 us -> none  [the longest x2 10.5 us: segment(): jnp.einsum('rs,rsw->rw', blend, features.reshape(slots, samples, width),...]
    all_gather x1 -> x0, blocking collectives: 20.3 us -> none  [gather_turned(): whole = lax.all_gather(both, axis, axis=0, tiled=True)]
    gather x1 -> x0, local copies, waits for them, and re-layouts: 16.9 us -> none  [forward(): hidden = table[cells.reshape(-1)]]
    unnamed x39 -> x8, local copies, waits for them, and re-layouts: 11.5 us -> 4.82 us
    reduce_sum x7 -> x0, other arithmetic: 4.71 us -> none  [the longest x1 3.4 us: on_device(): offset_grad = jnp.sum(grad_linear, axis=0)]
  transfers between devices with their start and end apart: 2 -> 0, of which waited for: 1 -> 0; matrix products, arithmetic and copies ran while one was open for 4% -> 0% of each run, Pallas kernels for 0% -> 0%
where the time goes in v1:
time: 59.6 us; the launch traced here: 59 us
  Pallas kernels  53.5 us (90%)
  local copies, waits for them, and re-layouts  4.82 us (8%)
  between operations  0.66 us (1%)
    pallas_call x1, Pallas kernels, on_device(): pl.pallas_call(kernel, out_shape=(jax.ShapeDtypeStruct((RAYS // PARTS, W)...  53.5 us
    unnamed x8, local copies, waits for them, and re-layouts  4.82 us

profile of v1, /device:TPU:8, one launch (start us, length us, event | category | flops | bytes accessed | tf_op | source)
XLA Modules:
  0.0 59.0 jit_solution(16746523556269301744)
XLA Ops:
  0.6 53.5 %shard_map.111 = (f32[32,256]{1,0:T(8,128)}, f32[4,256,256]{2,1,0:T(8,128)}, f32[4,256]{1,0:T(4,128)}, f32[1,256]{1,0:T(1,128)}) custom-call(s32[4096]{0:T(1024)} %bitcast.21, bf16[4096,256]{1,0:T(8,128)(2,1)} %bitcast.18, bf16[4,256,256]{2,1,0:T(8,128)(2,1)} %bitcast.19, f32[4,256]{1,0:T(4,128)} %bitcast.22, f32[1,256]{1,0:T(1,128)} %head.1, ...), custom_call_target="tpu_custom_call" | custom-call | flops 5905580032 | bytes 6291456 | tf_op jit(solution)/shard_map/pallas_call | solution.py:376
  54.2 0.0 copy-start
  54.2 0.0 copy-start.1
  54.2 1.4 %copy.16 = f32[32,256]{1,0:T(8,128)} copy(f32[32,256]{1,0:T(8,128)} %get-tuple-element.16) | data formatting | bytes 65536
  55.6 2.3 %copy.17 = f32[1,4,256,256]{3,2,1,0:T(8,128)} copy(f32[1,4,256,256]{3,2,1,0:T(8,128)} %bitcast.16) | data formatting | bytes 2097152
  57.9 0.0 copy-done
  57.9 0.6 %copy.18 = f32[1,4,256]{2,1,0:T(4,128)} copy(f32[1,4,256]{2,1,0:T(4,128)S(1)} %bitcast.17) | data formatting | bytes 8192
  58.5 0.0 copy-done.1
  58.5 0.6 copy.19
Async XLA Ops:
  54.2 3.7 %copy-start = (f32[4,256]{1,0:T(4,128)S(1)}, f32[4,256]{1,0:T(4,128)}, u32[]{:S(2)}) copy-start(f32[4,256]{1,0:T(4,128)} %get-tuple-element.10) | copy-start | bytes 12292
  54.2 4.3 %copy-start.1 = (f32[1,256]{1,0:T(1,128)S(1)}, f32[1,256]{1,0:T(1,128)}, u32[]{:S(2)}) copy-start(f32[1,256]{1,0:T(1,128)} %get-tuple-element.19) | copy-start | bytes 3076

commit v2 on v1

--- a/solution.py
+++ b/solution.py
@@ -25,6 +25,7 @@
 PARTS = 16
 SIDE = 4
 BLOCK = W // 2 // SIDE
+PART = BLOCK // SIDE
 UNROLL = 32
 
 
@@ -49,8 +50,9 @@
     comp_out, dw_out, bias_out, head_out,
     table32, rows32, x16, wt, cols, cot_t, hid, feat, grad, seg, colour, colour_rows,
     packed, gathered, comp_in, dw, col_sums, small, small_x, small_y,
-    red, in1, in2,
-    ag_send, ag_recv, comp_send, comp_recv, sends, recvs, small_send, small_recv,
+    in1, out1, red, in2,
+    ag_send, ag_recv, comp_send, comp_recv, sends, recvs, across_send, across_recv,
+    small_send, small_recv,
 ):
     space = lax.axis_index("space")
     ray = lax.axis_index("ray")
@@ -73,17 +75,19 @@
 
     def widen(k, _):
         part = table[pl.ds(pl.multiple_of(k * 512, 512), 512), :].astype(f32)
-        table32[pl.ds(pl.multiple_of(k * 512, 512), 512), 0, :] = part[:, :LANES]
-        table32[pl.ds(pl.multiple_of(k * 512, 512), 512), 1, :] = part[:, LANES:]
+        table32[pl.ds(pl.multiple_of(k * 1024, 1024), 512, stride=2), :] = part[:, :LANES]
+        table32[pl.ds(pl.multiple_of(k * 1024, 1024) + 1, 512, stride=2), :] = part[:, LANES:]
         return 0
 
     lax.fori_loop(0, CELLS // 512, widen, 0)
 
     def pick(k, _):
         base = k * UNROLL
-        got = [table32[cells[base + u]] for u in range(UNROLL)]
+        got = [
+            table32[pl.ds(2 * cells[base + u], 2), :] for u in range(UNROLL)
+        ]
         for u in range(UNROLL):
-            rows32[base + u] = got[u]
+            rows32[pl.ds(pl.multiple_of(2 * base, 2 * UNROLL) + 2 * u, 2), :] = got[u]
         return 0
 
     lax.fori_loop(0, SAMPLES // UNROLL, pick, 0)
@@ -97,9 +101,9 @@
     head_col = cols[:, LAYERS : LAYERS + 1] * ones
 
     def forward(c, _):
-        start = pl.multiple_of(c * CHUNK, CHUNK)
-        low = rows32[pl.ds(start, CHUNK), 0, :]
-        high = rows32[pl.ds(start, CHUNK), 1, :]
+        start = pl.multiple_of(c * 2 * CHUNK, 2 * CHUNK)
+        low = rows32[pl.ds(start, CHUNK, stride=2), :]
+        high = rows32[pl.ds(start + 1, CHUNK, stride=2), :]
         x = jnp.concatenate([low, high], axis=1).astype(bf16)
         x16[c] = x
         value = None
@@ -225,42 +229,119 @@
     col_sums[LAYERS] = head_sum
     col_sums[LAYERS - 1] = last_sum
 
-    def phase1(layer, half, d):
-        there, device = ray_peer(half, d)
+    def block_rows(half, d):
+        there = lax.rem(spot[half] + d + SIDE, SIDE)
+        return pl.ds(pl.multiple_of(half * (W // 2) + there * BLOCK, BLOCK), BLOCK)
+
+    def part_rows(half, d):
+        return pl.ds(pl.multiple_of(lax.rem(spot[1 - half] + d, SIDE) * PART, PART), PART)
+
+    sides = (pl.ds(0, LANES), pl.ds(LANES, LANES))
+    ways = (1, -1)
+
+    def step_copy(src, dst, layer, half, way, kind):
         return pltpu.make_async_remote_copy(
-            src_ref=dw.at[
-                layer, pl.ds(pl.multiple_of(half * (W // 2) + there * BLOCK, BLOCK), BLOCK), :
-            ],
-            dst_ref=in1.at[layer, half, d],
-            send_sem=sends.at[0, layer, half, d],
-            recv_sem=recvs.at[0, layer, half, d],
-            device_id=device,
+            src_ref=src,
+            dst_ref=dst,
+            send_sem=sends.at[layer, half, way, kind],
+            recv_sem=recvs.at[layer, half, way, kind],
+            device_id=ray_peer(half, ways[way] + SIDE)[1],
             device_id_type=MESH,
         )
 
-    def phase2(layer, half, d):
+    def far(layer, half, way):
+        src = dw.at[layer, block_rows(half, 2), sides[way]]
+        return step_copy(src, in1.at[layer, half, way, 0], layer, half, way, 0)
+
+    def near(layer, half, way):
+        src = dw.at[layer, block_rows(half, ways[way]), sides[1 - way]]
+        return step_copy(src, in1.at[layer, half, way, 1], layer, half, way, 1)
+
+    def joint(layer, half, way):
+        src = out1.at[layer, half, way]
+        return step_copy(src, in1.at[layer, half, way, 2], layer, half, way, 2)
+
+    def give(layer, half, way):
+        rows = dw_out.at[layer, block_rows(half, 0), :]
+        return step_copy(rows, rows, layer, half, way, 3)
+
+    def forward_on(layer, half, way):
+        rows = dw_out.at[layer, block_rows(half, -ways[way]), sides[way]]
+        return step_copy(rows, rows, layer, half, way, 4)
+
+    def across_copy(src, dst, layer, half, d, kind):
         return pltpu.make_async_remote_copy(
-            src_ref=red.at[layer, half],
-            dst_ref=in2.at[layer, half, spot[1 - half]],
-            send_sem=sends.at[1, layer, half, d],
-            recv_sem=recvs.at[1, layer, half, d],
+            src_ref=src,
+            dst_ref=dst,
+            send_sem=across_send.at[layer, half, kind, d],
+            recv_sem=across_recv.at[layer, half, kind, d],
             device_id=ray_peer(1 - half, d)[1],
             device_id_type=MESH,
         )
 
-    def own_rows(half):
-        return pl.ds(pl.multiple_of(half * (W // 2) + spot[half] * BLOCK, BLOCK), BLOCK)
-
-    def phase3(layer, half, d):
-        rows = dw_out.at[layer, own_rows(half), :]
-        return pltpu.make_async_remote_copy(
-            src_ref=rows,
-            dst_ref=rows,
-            send_sem=sends.at[2, layer, half, d],
-            recv_sem=recvs.at[2, layer, half, d],
-            device_id=ray_peer(half, d)[1],
-            device_id_type=MESH,
-        )
+    def scatter(layer, half, d):
+        src = red.at[layer, half, part_rows(half, d), :]
+        return across_copy(src, in2.at[layer, half, d], layer, half, d, 0)
+
+    def own_part(half):
+        start = half * (W // 2) + spot[half] * BLOCK + spot[1 - half] * PART
+        return pl.ds(pl.multiple_of(start, PART), PART)
+
+    def spread(layer, half, d):
+        rows = dw_out.at[layer, own_part(half), :]
+        return across_copy(rows, rows, layer, half, d, 1)
+
+    def reduce_stage(stage, layer):
+        for half in (0, 1):
+            if stage == 0:
+                for copy in (far, near):
+                    for way in (0, 1):
+                        copy(layer, half, way).start()
+            if stage == 1:
+                for way in (0, 1):
+                    far(layer, half, way).wait_recv()
+                    out1[layer, half, way] = (
+                        in1[layer, half, way, 0] + dw[layer, block_rows(half, ways[way]), sides[way]]
+                    )
+                    joint(layer, half, way).start()
+            if stage == 2:
+                for way in (0, 1):
+                    near(layer, half, 1 - way).wait_recv()
+                    joint(layer, half, way).wait_recv()
+                    red[layer, half, :, sides[way]] = (
+                        dw[layer, block_rows(half, 0), sides[way]]
+                        + in1[layer, half, 1 - way, 1]
+                        + in1[layer, half, way, 2]
+                    )
+                for d in range(1, SIDE):
+                    scatter(layer, half, d).start()
+            if stage == 3:
+                total = red[layer, half, part_rows(half, 0), :]
+                for d in range(1, SIDE):
+                    scatter(layer, half, d).wait_recv()
+                    total = total + in2[layer, half, d]
+                dw_out[layer, own_part(half), :] = total
+                for d in range(1, SIDE):
+                    spread(layer, half, d).start()
+            if stage == 4:
+                for d in range(1, SIDE):
+                    spread(layer, half, d).wait_recv()
+                for way in (0, 1):
+                    give(layer, half, way).start()
+            if stage == 5:
+                for way in (0, 1):
+                    give(layer, half, way).wait_recv()
+                    forward_on(layer, half, way).start()
+            if stage == 6:
+                for way in (0, 1):
+                    forward_on(layer, half, way).wait_recv()
+            if stage == 7:
+                for way in (0, 1):
+                    for copy in (far, near, joint, give, forward_on):
+                        copy(layer, half, way).wait_send()
+                for d in range(1, SIDE):
+                    scatter(layer, half, d).wait_send()
+                    spread(layer, half, d).wait_send()
 
     def small_copy(axis, d):
         return pltpu.make_async_remote_copy(
@@ -280,9 +361,9 @@
                 term = dot(grad[c], x16[c], 1, 0)
             total = term if c == 0 else total + term
         dw[layer] = total if layer > 0 else total.T
-        for d in range(1, SIDE):
-            for half in (0, 1):
-                phase1(layer, half, d).start()
+        reduce_stage(0, layer)
+        if layer + 1 < LAYERS:
+            reduce_stage(1, layer + 1)
         if layer > 0:
             def back(c, acc):
                 pulled = jnp.where(hid[layer - 1, c] > 0, dot(w[layer], grad[c], 1, 0), 0.0)
@@ -306,64 +387,51 @@
     for d in range(1, SIDE):
         small_copy(0, d).start()
 
-    order = range(LAYERS - 1, -1, -1)
-    for layer in order:
-        for half in (0, 1):
-            total = dw[layer, own_rows(half), :]
+    for wave in range(2, LAYERS + 6):
+        for stage in range(6, 0, -1):
+            layer = LAYERS - 1 - (wave - stage)
+            if 0 <= layer < LAYERS and not (stage == 1 and layer > 0):
+                reduce_stage(stage, layer)
+        if wave == 2:
+            small_x[spot[0]] = small[...]
             for d in range(1, SIDE):
-                phase1(layer, half, d).wait_recv()
-                total = total + in1[layer, half, d]
-            red[layer, half] = total
-            in2[layer, half, spot[1 - half]] = total
+                small_copy(0, d).wait_recv()
+            small_x[SIDE] = (small_x[0] + small_x[1]) + (small_x[2] + small_x[3])
             for d in range(1, SIDE):
-                phase2(layer, half, d).start()
-
-    small_x[spot[0]] = small[...]
-    for d in range(1, SIDE):
-        small_copy(0, d).wait_recv()
-    small_x[SIDE] = (small_x[0] + small_x[1]) + (small_x[2] + small_x[3])
-    for d in range(1, SIDE):
-        small_copy(1, d).start()
-
-    for layer in order:
-        for half in (0, 1):
+                small_copy(1, d).start()
+        if wave == 4:
+            small_y[spot[1]] = small_x[SIDE]
             for d in range(1, SIDE):
-                phase2(layer, half, d).wait_recv()
-            total = (in2[layer, half, 0] + in2[layer, half, 1]) + (
-                in2[layer, half, 2] + in2[layer, half, 3]
-            )
-            dw_out[layer, own_rows(half), :] = total
-            for d in range(1, SIDE):
-                phase3(layer, half, d).start()
-
-    small_y[spot[1]] = small_x[SIDE]
-    for d in range(1, SIDE):
-        small_copy(1, d).wait_recv()
-    summed = (small_y[0] + small_y[1]) + (small_y[2] + small_y[3])
-    bias_out[...] = summed[:LAYERS, :]
-    head_out[...] = summed[LAYERS : LAYERS + 1, :]
-
-    comp_in[space] = colour_rows[pl.ds(pl.multiple_of(space * kept, kept), kept), :]
-    for d in range(1, PARTS):
-        comp_copy(d).wait_recv()
-    total = comp_in[0]
-    for q in range(1, PARTS):
-        total = total + comp_in[q]
-    comp_out[...] = total
-
-    for layer in order:
-        for half in (0, 1):
-            for d in range(1, SIDE):
-                phase3(layer, half, d).wait_recv()
+                small_copy(1, d).wait_recv()
+            summed = (small_y[0] + small_y[1]) + (small_y[2] + small_y[3])
+            bias_out[...] = summed[:LAYERS, :]
+            head_out[...] = summed[LAYERS : LAYERS + 1, :]
+        if wave == 6:
+            comp_in[space] = colour_rows[pl.ds(pl.multiple_of(space * kept, kept), kept), :]
+            for d in range(1, PARTS):
+                comp_copy(d).wait_recv()
+            total = comp_in[0]
+            for q in range(1, PARTS):
+                total = total + comp_in[q]
+            comp_out[...] = total
+
     for d in range(1, PARTS):
         ag_copy(d).wait_send()
         comp_copy(d).wait_send()
     for axis in (0, 1):
         for d in range(1, SIDE):
             small_copy(axis, d).wait_send()
-            for layer in order:
-                for phase in (phase1, phase2, phase3):
-                    phase(layer, axis, d).wait_send()
+    for layer in range(LAYERS):
+        reduce_stage(7, layer)
+
+
+def hand_out(*refs):
+    sems = refs[8]
+    copies = [pltpu.make_async_copy(refs[k], refs[4 + k], sems.at[k]) for k in (1, 0, 2, 3)]
+    for copy in copies:
+        copy.start()
+    for copy in copies:
+        copy.wait()
 
 
 def on_device(
@@ -376,16 +444,16 @@
     composite, dw, db, dh = pl.pallas_call(
         kernel,
         out_shape=(
-            jax.ShapeDtypeStruct((RAYS // PARTS, W), f32),
-            jax.ShapeDtypeStruct((LAYERS, W, W), f32),
-            jax.ShapeDtypeStruct((LAYERS, W), f32),
-            jax.ShapeDtypeStruct((1, W), f32),
+            pltpu.VMEM((RAYS // PARTS, W), f32),
+            pltpu.VMEM((LAYERS, W, W), f32),
+            pltpu.VMEM((LAYERS, W), f32),
+            pltpu.VMEM((1, W), f32),
         ),
         in_specs=[pl.BlockSpec(memory_space=pltpu.SMEM)] + [in_vmem] * 7,
         out_specs=(in_vmem,) * 4,
         scratch_shapes=[
-            pltpu.VMEM((CELLS, 2, LANES), f32),
-            pltpu.VMEM((SAMPLES, 2, LANES), f32),
+            pltpu.VMEM((2 * CELLS, LANES), f32),
+            pltpu.VMEM((2 * SAMPLES, LANES), f32),
             pltpu.VMEM((CHUNKS, CHUNK, W), bf16),
             pltpu.VMEM((LAYERS, W, W), bf16),
             pltpu.VMEM((W, 8), f32),
@@ -404,15 +472,18 @@
             pltpu.VMEM((8, W), f32),
             pltpu.VMEM((SIDE + 1, 8, W), f32),
             pltpu.VMEM((SIDE, 8, W), f32),
+            pltpu.VMEM((LAYERS, 2, 2, 3, BLOCK, LANES), f32),
+            pltpu.VMEM((LAYERS, 2, 2, BLOCK, LANES), f32),
             pltpu.VMEM((LAYERS, 2, BLOCK, W), f32),
-            pltpu.VMEM((LAYERS, 2, SIDE, BLOCK, W), f32),
-            pltpu.VMEM((LAYERS, 2, SIDE, BLOCK, W), f32),
+            pltpu.VMEM((LAYERS, 2, SIDE, PART, W), f32),
             dma((PARTS,)),
             dma((PARTS,)),
             dma((PARTS,)),
             dma((PARTS,)),
-            dma((3, LAYERS, 2, SIDE)),
-            dma((3, LAYERS, 2, SIDE)),
+            dma((LAYERS, 2, 2, 5)),
+            dma((LAYERS, 2, 2, 5)),
+            dma((LAYERS, 2, 2, SIDE)),
+            dma((LAYERS, 2, 2, SIDE)),
             dma((2, SIDE)),
             dma((2, SIDE)),
         ],
@@ -425,6 +496,14 @@
     )(
         cells, grid_table[0], weights[0], biases[0], density_head, counts, ray_order.T, cotangent
     )
+    parts = (composite, dw, db, dh)
+    composite, dw, db, dh = pl.pallas_call(
+        hand_out,
+        out_shape=tuple(jax.ShapeDtypeStruct(p.shape, f32) for p in parts),
+        in_specs=[in_vmem] * 4,
+        out_specs=(pl.BlockSpec(memory_space=pl.ANY),) * 4,
+        scratch_shapes=[dma((4,))],
+    )(*(pltpu.with_memory_space_constraint(p, pltpu.VMEM) for p in parts))
     return composite, dw[None], db[None], dh
 
 

time: 59.6 us -> 64.4 us (1.081)
  Pallas kernels: 53.5 us -> 63.6 us
  local copies, waits for them, and re-layouts: 4.82 us -> 0 us
    pallas_call x1 -> x2, Pallas kernels: 53.5 us -> 63.6 us  [the longest x1 62.6 us: on_device(): pl.pallas_call(kernel, out_shape=(pltpu.VMEM((RAYS // PARTS, W), f32), pl...]
    unnamed x8 -> x0, local copies, waits for them, and re-layouts: 4.82 us -> none
where the time goes in v2:
time: 64.4 us; the launch traced here: 64.3 us
  Pallas kernels  63.6 us (99%)
    pallas_call x1, Pallas kernels, on_device(): pl.pallas_call(kernel, out_shape=(pltpu.VMEM((RAYS // PARTS, W), f32), pl...  62.6 us

profile of v2, /device:TPU:8, one launch (start us, length us, event | category | flops | bytes accessed | tf_op | source)
XLA Modules:
  0.0 64.3 jit_solution(1427802996686763032)
XLA Ops:
  0.6 62.6 %shard_map.111 = (f32[32,256]{1,0:T(8,128)S(1)}, f32[4,256,256]{2,1,0:T(8,128)S(1)}, f32[4,256]{1,0:T(4,128)S(1)}, f32[1,256]{1,0:T(1,128)S(1)}) custom-call(s32[4096]{0:T(1024)} %bitcast.20, bf16[4096,256]{1,0:T(8,128)(2,1)} %bitcast.16, bf16[4,256,256]{2,1,0:T(8,128)(2,1)} %bitcast.18, f32[4,256]{1,0:T(4,128)} %bitcast.21, f32[1,256]{1,0:T(1,128)} %head.1, ...), custom_call_target="tpu_custom_call" | custom-call | flops 5905580032 | bytes 6291456 | tf_op jit(solution)/shard_map/pallas_call | solution.py:444
  63.3 1.0 %shard_map.112 = (f32[32,256]{1,0:T(8,128)}, f32[4,256,256]{2,1,0:T(8,128)}, f32[4,256]{1,0:T(4,128)}, f32[1,256]{1,0:T(1,128)}) custom-call(f32[32,256]{1,0:T(8,128)S(1)} %get-tuple-element.12.refs_0_, f32[4,256,256]{2,1,0:T(8,128)S(1)} %get-tuple-element.13.refs_1_, f32[4,256]{1,0:T(4,128)S(1)} %get-tuple-element.14.refs_2_, ...), custom_call_target="tpu_custom_call" | custom-call | tf_op jit(solution)/shard_map/pallas_call | solution.py:500

commit v3 on v1

--- a/solution.py
+++ b/solution.py
@@ -26,6 +26,8 @@
 SIDE = 4
 BLOCK = W // 2 // SIDE
 UNROLL = 32
+PIECES = 4
+PIECE = CELLS // PIECES
 
 
 def dot(a, b, ca, cb):
@@ -45,13 +47,25 @@
 
 
 def kernel(
-    cells, table, w, bias, head, counts, ranks, cot,
+    cells, table_hbm, w_hbm, bias, head, counts, ranks, cot_hbm,
     comp_out, dw_out, bias_out, head_out,
-    table32, rows32, x16, wt, cols, cot_t, hid, feat, grad, seg, colour, colour_rows,
+    table, w, cot, fetch, table32, rows32, x16, wt, cols, cot_t, hid, feat, grad, seg, colour, colour_rows,
     packed, gathered, comp_in, dw, col_sums, small, small_x, small_y,
     red, in1, in2,
     ag_send, ag_recv, comp_send, comp_recv, sends, recvs, small_send, small_recv,
 ):
+    def piece(k):
+        rows = pl.ds(k * PIECE, PIECE)
+        return pltpu.make_async_copy(table_hbm.at[rows, :], table.at[rows, :], fetch.at[k])
+
+    others = (
+        pltpu.make_async_copy(w_hbm, w, fetch.at[PIECES]),
+        pltpu.make_async_copy(cot_hbm, cot, fetch.at[PIECES + 1]),
+    )
+    for k in range(PIECES):
+        piece(k).start()
+    for copy in others:
+        copy.start()
     space = lax.axis_index("space")
     ray = lax.axis_index("ray")
     spot = (ray // SIDE, ray % SIDE)
@@ -71,23 +85,31 @@
                 barrier, inc=1, device_id=ray_peer(axis, d)[1], device_id_type=MESH
             )
 
-    def widen(k, _):
-        part = table[pl.ds(pl.multiple_of(k * 512, 512), 512), :].astype(f32)
-        table32[pl.ds(pl.multiple_of(k * 512, 512), 512), 0, :] = part[:, :LANES]
-        table32[pl.ds(pl.multiple_of(k * 512, 512), 512), 1, :] = part[:, LANES:]
-        return 0
-
-    lax.fori_loop(0, CELLS // 512, widen, 0)
+    for k in range(PIECES):
+        piece(k).wait()
+
+        def widen(t, _):
+            start = pl.multiple_of(k * PIECE + t * 512, 512)
+            part = table[pl.ds(start, 512), :].astype(f32)
+            table32[pl.ds(pl.multiple_of(2 * start, 1024), 512, stride=2), :] = part[:, :LANES]
+            table32[pl.ds(pl.multiple_of(2 * start, 1024) + 1, 512, stride=2), :] = part[:, LANES:]
+            return 0
+
+        lax.fori_loop(0, PIECE // 512, widen, 0)
 
     def pick(k, _):
         base = k * UNROLL
-        got = [table32[cells[base + u]] for u in range(UNROLL)]
+        got = [
+            table32[pl.ds(2 * cells[base + u], 2), :] for u in range(UNROLL)
+        ]
         for u in range(UNROLL):
-            rows32[base + u] = got[u]
+            rows32[pl.ds(pl.multiple_of(2 * base, 2 * UNROLL) + 2 * u, 2), :] = got[u]
         return 0
 
-    lax.fori_loop(0, SAMPLES // UNROLL, pick, 0)
-
+    lax.fori_loop(0, GROUP // UNROLL, pick, 0)
+
+    for copy in others:
+        copy.wait()
     for layer in range(LAYERS):
         wt[layer] = w[layer].T
     cols[...] = jnp.concatenate([bias[...], head[...], jnp.zeros((3, W), f32)], axis=0).T
@@ -96,36 +118,36 @@
     ones = jnp.ones((1, LANES), f32)
     head_col = cols[:, LAYERS : LAYERS + 1] * ones
 
-    def forward(c, _):
-        start = pl.multiple_of(c * CHUNK, CHUNK)
-        low = rows32[pl.ds(start, CHUNK), 0, :]
-        high = rows32[pl.ds(start, CHUNK), 1, :]
+    def forward(g, more):
+        start = pl.multiple_of(g * 2 * GROUP, 2 * GROUP)
+        low = rows32[pl.ds(start, GROUP, stride=2), :]
+        high = rows32[pl.ds(start + 1, GROUP, stride=2), :]
         x = jnp.concatenate([low, high], axis=1).astype(bf16)
-        x16[c] = x
+        half = pl.ds(pl.multiple_of((g % WIDE) * GROUP, GROUP), GROUP)
+        x16[g // WIDE, half, :] = x
         value = None
         for layer in range(LAYERS):
+            if more:
+                for u in range(layer * GROUP // LAYERS, (layer + 1) * GROUP // LAYERS):
+                    row = table32[pl.ds(2 * cells[(g + 1) * GROUP + u], 2), :]
+                    rows32[pl.ds(pl.multiple_of((g + 1) * 2 * GROUP, 2 * GROUP) + 2 * u, 2), :] = row
             value = dot(wt[layer], x, 1, 1 if layer == 0 else 0) + cols[:, layer : layer + 1]
             if layer + 1 < LAYERS:
                 x = jnp.maximum(value, 0.0).astype(bf16)
-                hid[layer, c] = x
-        feat[c] = value
-        return 0
-
-    lax.fori_loop(0, CHUNKS, forward, 0)
-
-    decay_rows, product_rows = [], []
-    for g in range(GROUPS):
-        lanes = slice(g * LANES, (g + 1) * LANES)
-        turned = cot_t[:, lanes]
+                hid[layer, g // WIDE, :, half] = x
+        feat[g // WIDE, :, half] = value
+
+    def segment(g):
+        turned = cot_t[:, pl.ds(pl.multiple_of(g * LANES, LANES), LANES)]
         logit, along = [], []
         for s in range(SLOTS):
-            at = (g % WIDE) * GROUP + s * LANES
-            f = feat[g // WIDE, :, at : at + LANES]
+            at = pl.multiple_of((g % WIDE) * GROUP, GROUP) + s * LANES
+            f = feat[g // WIDE, :, pl.ds(at, LANES)]
             logit.append(jnp.sum(f * head_col, axis=0, keepdims=True))
             along.append(jnp.sum(f * turned, axis=0, keepdims=True))
         logit = jnp.concatenate(logit, axis=0)
         along = jnp.concatenate(along, axis=0)
-        live = slot_row < counts[g : g + 1, :]
+        live = slot_row < counts[pl.ds(g, 1), :]
         density = jnp.maximum(logit, 0.0) + jnp.log1p(jnp.exp(-jnp.abs(logit)))
         optical = jnp.where(live, density * STEP, 0.0)
         total = scan_down(optical, slot_row)
@@ -137,9 +159,14 @@
         seg[g, 0] = blend
         seg[g, 1] = along * through * past - (after - share)
         seg[g, 2] = jnp.where(live, STEP / (1.0 + jnp.exp(-logit)), 0.0)
-        decay_rows.append(-total[SLOTS - 1 : SLOTS, :])
-        product_rows.append(after[0:1, :])
-    packed[...] = jnp.concatenate(decay_rows + product_rows, axis=0)
+        packed[pl.ds(g, 1), :] = -total[SLOTS - 1 : SLOTS, :]
+        packed[pl.ds(GROUPS + g, 1), :] = after[0:1, :]
+
+    for g in range(GROUPS):
+        forward(g, g + 1 < GROUPS)
+        if g > 0:
+            segment(g - 1)
+    segment(GROUPS - 1)
 
     pl.semaphore_wait(barrier, PARTS - 1 + 2 * (SIDE - 1))
     mine = pl.multiple_of(space * 8, 8)
@@ -366,26 +393,42 @@
                     phase(layer, axis, d).wait_send()
 
 
+def hand_out(*refs):
+    sems = refs[8]
+    copies = [pltpu.make_async_copy(refs[k], refs[4 + k], sems.at[k]) for k in (1, 0, 2, 3)]
+    for copy in copies:
+        copy.start()
+    for copy in copies:
+        copy.wait()
+
+
 def on_device(
     grid_table, weights, biases, density_head, sample_cells, sample_counts, ray_order, cotangent
 ):
     cells = sample_cells[0].T.reshape(SLOTS, GROUPS, LANES).transpose(1, 0, 2).reshape(SAMPLES)
     counts = sample_counts.reshape(GROUPS, LANES)
     in_vmem = pl.BlockSpec(memory_space=pltpu.VMEM)
+    in_hbm = pl.BlockSpec(memory_space=pl.ANY)
     dma = pltpu.SemaphoreType.DMA
     composite, dw, db, dh = pl.pallas_call(
         kernel,
         out_shape=(
-            jax.ShapeDtypeStruct((RAYS // PARTS, W), f32),
-            jax.ShapeDtypeStruct((LAYERS, W, W), f32),
-            jax.ShapeDtypeStruct((LAYERS, W), f32),
-            jax.ShapeDtypeStruct((1, W), f32),
+            pltpu.VMEM((RAYS // PARTS, W), f32),
+            pltpu.VMEM((LAYERS, W, W), f32),
+            pltpu.VMEM((LAYERS, W), f32),
+            pltpu.VMEM((1, W), f32),
         ),
-        in_specs=[pl.BlockSpec(memory_space=pltpu.SMEM)] + [in_vmem] * 7,
+        in_specs=[
+            pl.BlockSpec(memory_space=pltpu.SMEM), in_hbm, in_hbm, in_vmem, in_vmem, in_vmem, in_vmem, in_hbm
+        ],
         out_specs=(in_vmem,) * 4,
         scratch_shapes=[
-            pltpu.VMEM((CELLS, 2, LANES), f32),
-            pltpu.VMEM((SAMPLES, 2, LANES), f32),
+            pltpu.VMEM((CELLS, W), bf16),
+            pltpu.VMEM((LAYERS, W, W), bf16),
+            pltpu.VMEM((RAYS, W), f32),
+            dma((PIECES + 2,)),
+            pltpu.VMEM((2 * CELLS, LANES), f32),
+            pltpu.VMEM((2 * SAMPLES, LANES), f32),
             pltpu.VMEM((CHUNKS, CHUNK, W), bf16),
             pltpu.VMEM((LAYERS, W, W), bf16),
             pltpu.VMEM((W, 8), f32),
@@ -425,6 +468,14 @@
     )(
         cells, grid_table[0], weights[0], biases[0], density_head, counts, ray_order.T, cotangent
     )
+    parts = (composite, dw, db, dh)
+    composite, dw, db, dh = pl.pallas_call(
+        hand_out,
+        out_shape=tuple(jax.ShapeDtypeStruct(p.shape, f32) for p in parts),
+        in_specs=[in_vmem] * 4,
+        out_specs=(pl.BlockSpec(memory_space=pl.ANY),) * 4,
+        scratch_shapes=[dma((4,))],
+    )(*(pltpu.with_memory_space_constraint(p, pltpu.VMEM) for p in parts))
     return composite, dw[None], db[None], dh
 
 

time: 59.6 us -> 49.2 us (0.83)
  Pallas kernels: 53.5 us -> 47.9 us
  local copies, waits for them, and re-layouts: 4.82 us -> 0 us
    pallas_call x1 -> x2, Pallas kernels: 53.5 us -> 47.9 us  [the longest x1 46.8 us: on_device(): pl.pallas_call(kernel, out_shape=(pltpu.VMEM((RAYS // PARTS, W), f32), pl...]
    unnamed x8 -> x0, local copies, waits for them, and re-layouts: 4.82 us -> none
where the time goes in v3:
time: 49.2 us; the launch traced here: 48.7 us
  Pallas kernels  47.9 us (97%)
  between operations  0.8 us (2%)
    pallas_call x1, Pallas kernels, on_device(): pl.pallas_call(kernel, out_shape=(pltpu.VMEM((RAYS // PARTS, W), f32), pl...  46.8 us
    pallas_call x1, Pallas kernels, on_device(): pl.pallas_call(hand_out, out_shape=tuple((jax.ShapeDtypeStruct(p.shape, f...  1.01 us

profile of v3, /device:TPU:8, one launch (start us, length us, event | category | flops | bytes accessed | tf_op | source)
XLA Modules:
  0.0 48.7 jit_solution(13384992871555545696)
XLA Ops:
  0.6 46.8 %shard_map.111 = (f32[32,256]{1,0:T(8,128)S(1)}, f32[4,256,256]{2,1,0:T(8,128)S(1)}, f32[4,256]{1,0:T(4,128)S(1)}, f32[1,256]{1,0:T(1,128)S(1)}) custom-call(s32[4096]{0:T(1024)} %bitcast.20, bf16[4096,256]{1,0:T(8,128)(2,1)} %bitcast.16, bf16[4,256,256]{2,1,0:T(8,128)(2,1)} %bitcast.18, f32[4,256]{1,0:T(4,128)} %bitcast.21, f32[1,256]{1,0:T(1,128)} %head.1, ...), custom_call_target="tpu_custom_call" | custom-call | flops 5905580032 | bytes 6291456 | tf_op jit(solution)/shard_map/pallas_call | solution.py:413
  47.5 1.0 %shard_map.112 = (f32[32,256]{1,0:T(8,128)}, f32[4,256,256]{2,1,0:T(8,128)}, f32[4,256]{1,0:T(4,128)}, f32[1,256]{1,0:T(1,128)}) custom-call(f32[32,256]{1,0:T(8,128)S(1)} %get-tuple-element.12.refs_0_, f32[4,256,256]{2,1,0:T(8,128)S(1)} %get-tuple-element.13.refs_1_, f32[4,256]{1,0:T(4,128)S(1)} %get-tuple-element.14.refs_2_, ...), custom_call_target="tpu_custom_call" | custom-call | tf_op jit(solution)/shard_map/pallas_call | solution.py:472

commit v4 on v3

--- a/solution.py
+++ b/solution.py
@@ -19,15 +19,13 @@
 GROUPS = RAYS // LANES
 GROUP = SLOTS * LANES
 SAMPLES = RAYS * SLOTS
-WIDE = 2
+WIDE = 4
 CHUNKS = GROUPS // WIDE
 CHUNK = WIDE * GROUP
 PARTS = 16
 SIDE = 4
 BLOCK = W // 2 // SIDE
 UNROLL = 32
-PIECES = 4
-PIECE = CELLS // PIECES
 
 
 def dot(a, b, ca, cb):
@@ -47,25 +45,13 @@
 
 
 def kernel(
-    cells, table_hbm, w_hbm, bias, head, counts, ranks, cot_hbm,
+    cells, table, w, bias, head, counts, ranks, cot,
     comp_out, dw_out, bias_out, head_out,
-    table, w, cot, fetch, table32, rows32, x16, wt, cols, cot_t, hid, feat, grad, seg, colour, colour_rows,
+    table32, rows32, x16, wt, cols, cot_t, hid, feat, grad, seg, colour, colour_rows,
     packed, gathered, comp_in, dw, col_sums, small, small_x, small_y,
     red, in1, in2,
     ag_send, ag_recv, comp_send, comp_recv, sends, recvs, small_send, small_recv,
 ):
-    def piece(k):
-        rows = pl.ds(k * PIECE, PIECE)
-        return pltpu.make_async_copy(table_hbm.at[rows, :], table.at[rows, :], fetch.at[k])
-
-    others = (
-        pltpu.make_async_copy(w_hbm, w, fetch.at[PIECES]),
-        pltpu.make_async_copy(cot_hbm, cot, fetch.at[PIECES + 1]),
-    )
-    for k in range(PIECES):
-        piece(k).start()
-    for copy in others:
-        copy.start()
     space = lax.axis_index("space")
     ray = lax.axis_index("ray")
     spot = (ray // SIDE, ray % SIDE)
@@ -85,17 +71,13 @@
                 barrier, inc=1, device_id=ray_peer(axis, d)[1], device_id_type=MESH
             )
 
-    for k in range(PIECES):
-        piece(k).wait()
-
-        def widen(t, _):
-            start = pl.multiple_of(k * PIECE + t * 512, 512)
-            part = table[pl.ds(start, 512), :].astype(f32)
-            table32[pl.ds(pl.multiple_of(2 * start, 1024), 512, stride=2), :] = part[:, :LANES]
-            table32[pl.ds(pl.multiple_of(2 * start, 1024) + 1, 512, stride=2), :] = part[:, LANES:]
-            return 0
-
-        lax.fori_loop(0, PIECE // 512, widen, 0)
+    def widen(k, _):
+        part = table[pl.ds(pl.multiple_of(k * 512, 512), 512), :].astype(f32)
+        table32[pl.ds(pl.multiple_of(k * 1024, 1024), 512, stride=2), :] = part[:, :LANES]
+        table32[pl.ds(pl.multiple_of(k * 1024, 1024) + 1, 512, stride=2), :] = part[:, LANES:]
+        return 0
+
+    lax.fori_loop(0, CELLS // 512, widen, 0)
 
     def pick(k, _):
         base = k * UNROLL
@@ -108,8 +90,6 @@
 
     lax.fori_loop(0, GROUP // UNROLL, pick, 0)
 
-    for copy in others:
-        copy.wait()
     for layer in range(LAYERS):
         wt[layer] = w[layer].T
     cols[...] = jnp.concatenate([bias[...], head[...], jnp.zeros((3, W), f32)], axis=0).T
@@ -408,7 +388,6 @@
     cells = sample_cells[0].T.reshape(SLOTS, GROUPS, LANES).transpose(1, 0, 2).reshape(SAMPLES)
     counts = sample_counts.reshape(GROUPS, LANES)
     in_vmem = pl.BlockSpec(memory_space=pltpu.VMEM)
-    in_hbm = pl.BlockSpec(memory_space=pl.ANY)
     dma = pltpu.SemaphoreType.DMA
     composite, dw, db, dh = pl.pallas_call(
         kernel,
@@ -418,15 +397,9 @@
             pltpu.VMEM((LAYERS, W), f32),
             pltpu.VMEM((1, W), f32),
         ),
-        in_specs=[
-            pl.BlockSpec(memory_space=pltpu.SMEM), in_hbm, in_hbm, in_vmem, in_vmem, in_vmem, in_vmem, in_hbm
-        ],
+        in_specs=[pl.BlockSpec(memory_space=pltpu.SMEM)] + [in_vmem] * 7,
         out_specs=(in_vmem,) * 4,
         scratch_shapes=[
-            pltpu.VMEM((CELLS, W), bf16),
-            pltpu.VMEM((LAYERS, W, W), bf16),
-            pltpu.VMEM((RAYS, W), f32),
-            dma((PIECES + 2,)),
             pltpu.VMEM((2 * CELLS, LANES), f32),
             pltpu.VMEM((2 * SAMPLES, LANES), f32),
             pltpu.VMEM((CHUNKS, CHUNK, W), bf16),

time: 49.2 us -> 47.3 us (0.961)
  Pallas kernels: 47.9 us -> 46 us
    pallas_call x1, Pallas kernels: 46.8 us -> 45 us  [on_device(): pl.pallas_call(kernel, out_shape=(pltpu.VMEM((RAYS // PARTS, W), f32), pl...]
where the time goes in v4:
time: 47.3 us; the launch traced here: 46.8 us
  Pallas kernels  46 us (97%)
  between operations  0.8 us (2%)
    pallas_call x1, Pallas kernels, on_device(): pl.pallas_call(kernel, out_shape=(pltpu.VMEM((RAYS // PARTS, W), f32), pl...  45 us
    pallas_call x1, Pallas kernels, on_device(): pl.pallas_call(hand_out, out_shape=tuple((jax.ShapeDtypeStruct(p.shape, f...  1.01 us

profile of v4, /device:TPU:8, one launch (start us, length us, event | category | flops | bytes accessed | tf_op | source)
XLA Modules:
  0.0 46.8 jit_solution(15015192310924690383)
XLA Ops:
  0.6 45.0 %shard_map.111 = (f32[32,256]{1,0:T(8,128)S(1)}, f32[4,256,256]{2,1,0:T(8,128)S(1)}, f32[4,256]{1,0:T(4,128)S(1)}, f32[1,256]{1,0:T(1,128)S(1)}) custom-call(s32[4096]{0:T(1024)} %bitcast.20, bf16[4096,256]{1,0:T(8,128)(2,1)} %bitcast.16, bf16[4,256,256]{2,1,0:T(8,128)(2,1)} %bitcast.18, f32[4,256]{1,0:T(4,128)} %bitcast.21, f32[1,256]{1,0:T(1,128)} %head.1, ...), custom_call_target="tpu_custom_call" | custom-call | flops 5905580032 | bytes 6291456 | tf_op jit(solution)/shard_map/pallas_call | solution.py:392
  45.6 1.0 %shard_map.112 = (f32[32,256]{1,0:T(8,128)}, f32[4,256,256]{2,1,0:T(8,128)}, f32[4,256]{1,0:T(4,128)}, f32[1,256]{1,0:T(1,128)}) custom-call(f32[32,256]{1,0:T(8,128)S(1)} %get-tuple-element.12.refs_0_, f32[4,256,256]{2,1,0:T(8,128)S(1)} %get-tuple-element.13.refs_1_, f32[4,256]{1,0:T(4,128)S(1)} %get-tuple-element.14.refs_2_, ...), custom_call_target="tpu_custom_call" | custom-call | tf_op jit(solution)/shard_map/pallas_call | solution.py:445

commit v5 on v4

--- a/solution.py
+++ b/solution.py
@@ -303,18 +303,18 @@
                 acc = back(c, acc)
             col_sums[layer - 1] = acc
 
-    lane = lax.broadcasted_iota(jnp.int32, (W, LANES), 1)
-    gathered_cols = jnp.zeros((W, LANES), f32)
-    for k in range(LAYERS + 1):
-        gathered_cols = jnp.where(
-            lane == k, jnp.sum(col_sums[k], axis=1, keepdims=True), gathered_cols
-        )
-    small[...] = gathered_cols.T[:8, :]
-    for d in range(1, SIDE):
-        small_copy(0, d).start()
-
     order = range(LAYERS - 1, -1, -1)
     for layer in order:
+        if layer == 0:
+            lane = lax.broadcasted_iota(jnp.int32, (W, LANES), 1)
+            gathered_cols = jnp.zeros((W, LANES), f32)
+            for k in range(LAYERS + 1):
+                gathered_cols = jnp.where(
+                    lane == k, jnp.sum(col_sums[k], axis=1, keepdims=True), gathered_cols
+                )
+            small[...] = gathered_cols.T[:8, :]
+            for d in range(1, SIDE):
+                small_copy(0, d).start()
         for half in (0, 1):
             total = dw[layer, own_rows(half), :]
             for d in range(1, SIDE):

time: 47.3 us -> 48.6 us (1.027)
  Pallas kernels: 46 us -> 47.1 us
    pallas_call x1, Pallas kernels: 45 us -> 46.1 us  [on_device(): pl.pallas_call(kernel, out_shape=(pltpu.VMEM((RAYS // PARTS, W), f32), pl...]
where the time goes in v5:
time: 48.6 us; the launch traced here: 47.9 us
  Pallas kernels  47.1 us (97%)
  between operations  0.8 us (2%)
    pallas_call x1, Pallas kernels, on_device(): pl.pallas_call(kernel, out_shape=(pltpu.VMEM((RAYS // PARTS, W), f32), pl...  46.1 us
    pallas_call x1, Pallas kernels, on_device(): pl.pallas_call(hand_out, out_shape=tuple((jax.ShapeDtypeStruct(p.shape, f...  1.01 us

profile of v5, /device:TPU:8, one launch (start us, length us, event | category | flops | bytes accessed | tf_op | source)
XLA Modules:
  0.0 47.9 jit_solution(7407916750629210797)
XLA Ops:
  0.6 46.1 %shard_map.111 = (f32[32,256]{1,0:T(8,128)S(1)}, f32[4,256,256]{2,1,0:T(8,128)S(1)}, f32[4,256]{1,0:T(4,128)S(1)}, f32[1,256]{1,0:T(1,128)S(1)}) custom-call(s32[4096]{0:T(1024)} %bitcast.20, bf16[4096,256]{1,0:T(8,128)(2,1)} %bitcast.16, bf16[4,256,256]{2,1,0:T(8,128)(2,1)} %bitcast.18, f32[4,256]{1,0:T(4,128)} %bitcast.21, f32[1,256]{1,0:T(1,128)} %head.1, ...), custom_call_target="tpu_custom_call" | custom-call | flops 5905580032 | bytes 6291456 | tf_op jit(solution)/shard_map/pallas_call | solution.py:392
  46.7 1.0 %shard_map.112 = (f32[32,256]{1,0:T(8,128)}, f32[4,256,256]{2,1,0:T(8,128)}, f32[4,256]{1,0:T(4,128)}, f32[1,256]{1,0:T(1,128)}) custom-call(f32[32,256]{1,0:T(8,128)S(1)} %get-tuple-element.12.refs_0_, f32[4,256,256]{2,1,0:T(8,128)S(1)} %get-tuple-element.13.refs_1_, f32[4,256]{1,0:T(4,128)S(1)} %get-tuple-element.14.refs_2_, ...), custom_call_target="tpu_custom_call" | custom-call | tf_op jit(solution)/shard_map/pallas_call | solution.py:445
